TPU v7x, 256 devices: a whole 4x4x8 slice. The times are simulated.
256 devices in a mesh: snap: 64 (over z, y, core), rep: 4 (over x).
Axes of the slice: x: 4, y: 4, z: 8, core: 2. Of those that a mesh axis runs over, the one named last changes fastest.
Arguments:
- features: float32 [64, 8192, 256], P('snap', 'rep'), parts along dimension 1, may hold values from -6 to 6
- tiles: float32 [64, 128, 128, 128], P('snap', 'rep'), parts along dimension 1, may hold values from -0.375 to 0.375
- coords: int32 [64, 128, 2], P('snap', 'rep'), parts along dimension 1, may hold values from -1 to 15, as said below
- temporal: float32 [64, 64], replicated, may hold values from 0 to 2, as said below
- weight_one: float32 [256, 256], replicated, may hold values from -0.375 to 0.375
- weight_two: float32 [256, 256], replicated, may hold values from -0.375 to 0.375
Outputs:
- hidden_two: float32 [64, 8192, 256], P('snap', 'rep'), parts along dimension 1
There are 4 independent parts, one for each index of `rep`. A program takes and returns all parts, laid end to end along the dimension named above; an argument that names none is the same for every part. Nothing has to cross between parts.
Inputs may be any that keep to these rules, and one draw needn't show every extreme that they name: `coords`: each snapshot lists at most 32 distinct tiles (row block, column block) in its first slots; the remaining slots hold -1 in both entries; some snapshot uses all 32 slots. `temporal`: zero above the diagonal.
All inputs are finite; a program needn't handle non-finite values.
Results may differ from a plain program's by a relative error of at most 0.0003.
Values sent between devices are 32-bit elements; how exact they have to be, the bound alone decides.
No kernel may reach another device: no remote copies, remote signals or barrier semaphores. Data moves between devices by JAX's collectives and lax.ppermute only.
A program may use at most 64 MiB of HBM per device.

v0:
```python
import jax
import jax.numpy as jnp
from jax import lax
from jax.sharding import PartitionSpec as P


def tile_block(hblocks, tile_vals, tile_coords):
    nblocks = hblocks.shape[0]
    is_used = tile_coords[:, 0] >= 0
    col_index = jnp.where(is_used, tile_coords[:, 1], 0)
    gathered = hblocks[col_index]
    products = jnp.einsum("kij,kjf->kif", tile_vals, gathered, precision=lax.Precision.HIGHEST)
    one_hot = (tile_coords[:, 0][None, :] == jnp.arange(nblocks, dtype=jnp.int32)[:, None]).astype(
        jnp.float32
    )
    return jnp.einsum("rk,kif->rif", one_hot, products, precision=lax.Precision.HIGHEST)


def local_products(state, tiles, coords):
    snap_count, vert_count, feat_count = state.shape
    tile_len = tiles.shape[2]
    nblocks = vert_count // tile_len
    hblocks = state.reshape(snap_count, nblocks, tile_len, feat_count)
    summed = jax.vmap(tile_block)(hblocks, tiles, coords)
    return summed.reshape(snap_count, vert_count, feat_count)


def apply_weight(values, weight):
    flat = values.reshape(-1, values.shape[-1])
    return jnp.dot(flat, weight, precision=lax.Precision.HIGHEST).reshape(values.shape)


def shards(features, tiles, coords, temporal, weight_one, weight_two):
    state = features
    layer_weights = (weight_one, weight_two)
    for depth in range(2):
        summed = local_products(state, tiles, coords)
        projected = apply_weight(summed, layer_weights[depth])
        mixed = jnp.tanh(
            jnp.einsum(
                "ts,svk->tvk",
                temporal,
                lax.all_to_all(projected, "snap", split_axis=1, concat_axis=0, tiled=True),
                precision=lax.Precision.HIGHEST,
            )
        )
        state = lax.all_to_all(mixed, "snap", split_axis=0, concat_axis=1, tiled=True)
    return state


def solution(mesh):
    return jax.shard_map(
        shards,
        mesh=mesh,
        in_specs=(
            P("snap", "rep", None),
            P("snap", "rep", None, None),
            P("snap", "rep", None),
            P(),
            P(),
            P(),
        ),
        out_specs=P("snap", "rep", None),
        check_vma=False,
    )
```

profile of v0, /device:TPU:6, one launch (start us, length us, event | category | flops | bytes accessed | tf_op | source)
XLA Modules:
  0.0 317.5 jit_solution(1265702644759121901)
XLA Ops:
  0.9 4.4 %gather_fusion = f32[32,128,256]{2,1,0:T(8,128)} fusion(f32[1,16,128,256]{3,2,1,0:T(8,128)} %bitcast.48, s32[32]{0:T(128)S(1)} %or_bitcast_fusion), kind=kCustom, calls=%fused_computation | custom fusion | bytes 8388864 | tf_op jit(solution)/shard_map/vmap()/gather | solution.py:11
  5.3 10.4 %convolution_bitcast_fusion.3 = f32[32,128,256]{1,2,0:T(8,128)} fusion(f32[32,128,256]{2,1,0:T(8,128)} %gather_fusion, f32[1,32,128,128]{3,2,1,0:T(8,128)S(1)} %copy-done), kind=kOutput, calls=%fused_computation.5 | convolution fusion | flops 1610612736 | bytes 10485760 | tf_op jit(solution)/shard_map/vmap(kij,kjf->kif)/dot_general | solution.py:12
  15.7 5.5 %copy.25 = f32[32,128,256]{2,0,1:T(8,128)} copy(f32[32,128,256]{1,2,0:T(8,128)} %convolution_bitcast_fusion.3) | data formatting | bytes 8388608 | tf_op jit(solution)/shard_map/vmap(kij,kjf->kif)/dot_general | solution.py:12
  21.2 3.8 %fusion.15 = f32[16,128,256]{2,0,1:T(8,128)S(1)} fusion(f32[32,128,256]{2,0,1:T(8,128)} %copy.25, s32[32]{0:T(128)S(1)} %get-tuple-element.5), kind=kOutput, calls=%fused_computation.19 | convolution fusion | flops 201327104 | bytes 6291584 | tf_op jit(solution)/shard_map/vmap(rk,kif->rif)/dot_general | solution.py:16
  25.0 1.2 copy.26
  26.2 1.9 convolution_bitcast_fusion.1
  28.1 8.6 %copy.27 = f32[1,2048,256]{2,0,1:T(1,128)S(1)} copy(f32[1,2048,256]{2,1,0:T(8,128)S(1)} %convolution_bitcast_fusion.1) | data formatting | bytes 4194304 | tf_op jit(solution)/shard_map/reshape | solution.py:30
  36.7 63.3 %all_to_all.45 = f32[1,2048,256]{2,0,1:T(1,128)S(1)} all-to-all(f32[1,2048,256]{2,0,1:T(1,128)S(1)} %copy.27), channel_id=1, replica_groups=mesh['snap'=64,'rep'=4] {'snap'}, dimensions={1} | all-to-all | bytes 4194304 | tf_op jit(solution)/shard_map/all_to_all | solution.py:43
  100.7 3.3 %tanh_bitcast_fusion.1 = f32[64,32,256]{2,0,1:T(8,128)S(1)} fusion(f32[64,32,256]{2,1,0:T(8,128)S(1)} %bitcast.50, f32[64,64]{1,0:T(8,128)S(1)} %copy-done.4), kind=kOutput, calls=%fused_computation.13 | convolution fusion | flops 402653184 | bytes 4210688 | tf_op jit(solution)/shard_map/ts,svk->tvk/dot_general | solution.py:40
  104.0 1.2 copy.29
  105.2 56.6 %all_to_all.46 = f32[64,32,256]{2,1,0:T(8,128)} all-to-all(f32[64,32,256]{2,1,0:T(8,128)S(1)} %copy.29), channel_id=1, replica_groups=mesh['snap'=64,'rep'=4] {'snap'}, dimensions={0} | all-to-all | bytes 4194304 | tf_op jit(solution)/shard_map/all_to_all | solution.py:47
  161.8 4.3 %gather_fusion.1 = f32[32,128,256]{2,1,0:T(8,128)} fusion(f32[1,16,128,256]{3,2,1,0:T(8,128)} %bitcast.47, s32[32]{0:T(128)S(1)} %or_bitcast_fusion), kind=kCustom, calls=%fused_computation.1 | custom fusion | bytes 8388864 | tf_op jit(solution)/shard_map/vmap()/gather | solution.py:11
  166.2 10.5 %convolution_bitcast_fusion.2 = f32[32,128,256]{1,2,0:T(8,128)} fusion(f32[32,128,256]{2,1,0:T(8,128)} %gather_fusion.1, f32[1,32,128,128]{3,2,1,0:T(8,128)S(1)} %copy-done), kind=kOutput, calls=%fused_computation.4 | convolution fusion | flops 1610612736 | bytes 10485760 | tf_op jit(solution)/shard_map/vmap(kij,kjf->kif)/dot_general | solution.py:12
  176.6 5.5 %copy.31 = f32[32,128,256]{2,0,1:T(8,128)} copy(f32[32,128,256]{1,2,0:T(8,128)} %convolution_bitcast_fusion.2) | data formatting | bytes 8388608 | tf_op jit(solution)/shard_map/vmap(kij,kjf->kif)/dot_general | solution.py:12
  182.1 3.7 %fusion.13 = f32[16,128,256]{2,0,1:T(8,128)S(1)} fusion(f32[32,128,256]{2,0,1:T(8,128)} %copy.31, s32[32]{0:T(128)S(1)} %get-tuple-element.5), kind=kOutput, calls=%fused_computation.18 | convolution fusion | flops 201327104 | bytes 6291584 | tf_op jit(solution)/shard_map/vmap(rk,kif->rif)/dot_general | solution.py:16
  185.9 1.2 copy.32
  187.1 1.8 convolution_bitcast_fusion
  188.9 8.6 %copy.33 = f32[1,2048,256]{2,0,1:T(1,128)S(1)} copy(f32[1,2048,256]{2,1,0:T(8,128)S(1)} %convolution_bitcast_fusion) | data formatting | bytes 4194304 | tf_op jit(solution)/shard_map/reshape | solution.py:30
  197.5 56.5 %all_to_all.47 = f32[1,2048,256]{2,0,1:T(1,128)S(1)} all-to-all(f32[1,2048,256]{2,0,1:T(1,128)S(1)} %copy.33), channel_id=1, replica_groups=mesh['snap'=64,'rep'=4] {'snap'}, dimensions={1} | all-to-all | bytes 4194304 | tf_op jit(solution)/shard_map/all_to_all | solution.py:43
  254.2 3.3 %tanh_bitcast_fusion = f32[64,32,256]{2,0,1:T(8,128)S(1)} fusion(f32[64,32,256]{2,1,0:T(8,128)S(1)} %bitcast.52, f32[64,64]{1,0:T(8,128)S(1)} %copy-done.4), kind=kOutput, calls=%fused_computation.12 | convolution fusion | flops 402653184 | bytes 4210688 | tf_op jit(solution)/shard_map/ts,svk->tvk/dot_general | solution.py:40
  257.4 1.2 copy.35
  258.7 56.5 %all_to_all.48 = f32[64,32,256]{2,1,0:T(8,128)S(1)} all-to-all(f32[64,32,256]{2,1,0:T(8,128)S(1)} %copy.35), channel_id=1, replica_groups=mesh['snap'=64,'rep'=4] {'snap'}, dimensions={0} | all-to-all | bytes 4194304 | tf_op jit(solution)/shard_map/all_to_all | solution.py:47
  315.1 1.3 copy.49
  316.5 1.0 copy-done.1
  (14 shorter events, 1.8 us)
Async XLA Ops:
  0.0 5.3 %copy-start = (f32[1,32,128,128]{3,2,1,0:T(8,128)S(1)}, f32[1,32,128,128]{3,2,1,0:T(8,128)}, u32[]{:S(2)}) copy-start(f32[1,32,128,128]{3,2,1,0:T(8,128)} %param.7) | copy-start | bytes 6291460
  25.0 1.2 copy-start.2
  100.0 0.8 copy-start.4
  185.9 1.2 copy-start.3
  315.1 2.3 copy-start.1
where the time goes:
time: 318 us; the launch traced here: 317 us
  blocking collectives  233 us (73%)
  local copies, waits for them, and re-layouts  45 us (14%)
  matrix products  38.7 us (12%)
    all_to_all x2, blocking collectives, shards(): lax.all_to_all(projected, 'snap', split_axis=1, concat_axis=0, tiled=True)  120 us
    all_to_all x2, blocking collectives, shards(): lax.all_to_all(mixed, 'snap', split_axis=0, concat_axis=1, tiled=True)  113 us
    dot_general x2, matrix products, tile_block(): jnp.einsum('kij,kjf->kif', tile_vals, gathered, precision=lax.Precision.H...  20.9 us
    reshape x2, local copies, waits for them, and re-layouts, apply_weight(): jnp.dot(flat, weight, precision=lax.Precision.HIGHEST).reshape(values.shape)  17.1 us
    dot_general x2, local copies, waits for them, and re-layouts, tile_block(): jnp.einsum('kij,kjf->kif', tile_vals, gathered, precision=lax.Precision.H...  11 us
    gather x3, local copies, waits for them, and re-layouts, tile_block(): gathered = hblocks[col_index]  8.73 us
    dot_general x2, matrix products, tile_block(): jnp.einsum('rk,kif->rif', one_hot, products, precision=lax.Precision.HIGH...  7.51 us
    dot_general x2, matrix products, shards(): jnp.einsum('ts,svk->tvk', temporal, lax.all_to_all(projected, 'snap', spl...  6.54 us

commit v1 on v0

v1 whole, which is shorter than its diff:
```python
import jax
import jax.numpy as jnp
from jax import lax
from jax.experimental import pallas as pl
from jax.experimental.pallas import tpu as pltpu
from jax.sharding import PartitionSpec as P

SNAPS = 64
VERT, FEAT, TILE = 2048, 256, 128
HALF = FEAT // 2
OWN = VERT // SNAPS
NBLK = VERT // TILE
BF, F32 = jnp.bfloat16, jnp.float32
WHOLE = jax.ShapeDtypeStruct((SNAPS, OWN, FEAT), F32)
PARAMS = pltpu.CompilerParams(vmem_limit_bytes=32 * 1024 * 1024)
VSPEC = pl.BlockSpec(memory_space=pltpu.VMEM)
SSPEC = pl.BlockSpec(memory_space=pltpu.SMEM)


def split(x):
    hi = x.astype(BF)
    return hi, (x - hi.astype(F32)).astype(BF)


def dot(a, b):
    return jnp.dot(a, b, preferred_element_type=F32)


def put_block(pair, row, value):
    hi, lo = split(value)
    blk = row // TILE
    both = jnp.concatenate([hi, lo], axis=1)
    pair[blk, :TILE] = both
    pair[blk, TILE:] = both


def tile_products(coords, tiles, pair, acc):
    acc[...] = jnp.zeros_like(acc)
    count = tiles.shape[0]
    for k in range(count):
        row = coords[2 * k]
        used = row >= 0
        row = jnp.where(used, row, NBLK)
        col = jnp.where(used, coords[2 * k + 1], 0)
        hi, lo = split(tiles[k])
        wide = dot(jnp.concatenate([hi, lo], axis=1), pair[col])
        acc[row] += wide[:, :HALF] + wide[:, HALF:]


def product_kernel(coords, state, tiles, weight, out, pair, acc):
    for h in range(2):
        cols = slice(h * HALF, (h + 1) * HALF)
        w_hi, w_lo = split(weight[:, cols])
        for r in range(0, VERT, 256):
            s_hi, s_lo = split(state[r : r + 256, :])
            u = dot(s_hi, w_hi) + (dot(s_hi, w_lo) + dot(s_lo, w_hi))
            for q in range(0, 256, TILE):
                put_block(pair, r + q, u[q : q + TILE])
        tile_products(coords, tiles, pair, acc)
        out[:, :, cols] = acc[:NBLK].reshape(SNAPS, OWN, HALF)


SCRATCH = [pltpu.VMEM((NBLK, 2 * TILE, FEAT), BF), pltpu.VMEM((NBLK + 1, TILE, HALF), F32)]


def cost(flops, moved):
    return pl.CostEstimate(flops=flops, bytes_accessed=moved, transcendentals=0)


def call(kernel, name, out_shape, in_specs, scratch, flops, moved, *args):
    return pl.pallas_call(
        kernel,
        out_shape=out_shape,
        in_specs=in_specs,
        out_specs=jax.tree.map(lambda _: VSPEC, out_shape),
        scratch_shapes=scratch,
        compiler_params=PARAMS,
        cost_estimate=cost(flops, moved),
        name=name,
    )(*args)


def product(coords, state, tiles, weight):
    return call(
        product_kernel, "product", WHOLE, [SSPEC, VSPEC, VSPEC, VSPEC], SCRATCH,
        3_200_000_000, 6 << 20, coords, state, tiles, weight,
    )


def mix_kernel(mixer, part, out):
    t_hi, t_lo = split(mixer[...])
    lhs = jnp.concatenate([t_hi, t_lo, t_hi, t_lo], axis=1)
    for i in range(OWN):
        hi, lo = split(part[:, i, :])
        out[:, i, :] = jnp.tanh(dot(lhs, jnp.concatenate([hi, hi, lo, lo], axis=0)))


def mix(mixer, part):
    return call(mix_kernel, "mix", WHOLE, [VSPEC] * 2, [], 1_600_000_000, 4 << 20, mixer, part)


def exchange(x):
    return lax.all_to_all(x, "snap", split_axis=0, concat_axis=0, tiled=True)


def shards(features, tiles, coords, temporal, weight_one, weight_two):
    tiles = tiles.reshape(tiles.shape[1:])
    coords = coords.reshape(-1)
    state = features
    for weight in (weight_one, weight_two):
        mine = product(coords, state.reshape(VERT, FEAT), tiles, weight)
        state = exchange(mix(temporal, exchange(mine)))
    return state.reshape(features.shape)


def solution(mesh):
    return jax.shard_map(
        shards,
        mesh=mesh,
        in_specs=(
            P("snap", "rep", None),
            P("snap", "rep", None, None),
            P("snap", "rep", None),
            P(),
            P(),
            P(),
        ),
        out_specs=P("snap", "rep", None),
        check_vma=False,
    )
```

time: 318 us -> 262 us (0.82)
  matrix products: 38.7 us -> 0 us
  local copies, waits for them, and re-layouts: 45 us -> 6.33 us
  Pallas kernels: 0 us -> 22.6 us
    dot_general x8 -> x0, matrix products: 38.7 us -> none  [the longest x2 20.9 us: tile_block(): jnp.einsum('kij,kjf->kif', tile_vals, gathered, precision=lax.Precision.H...]
    pallas_call x0 -> x4, Pallas kernels: none -> 22.6 us  [call(): pl.pallas_call(kernel, out_shape=out_shape, in_specs=in_specs, out_specs=...]
    reshape x2 -> x1, local copies, waits for them, and re-layouts: 17.1 us -> 0.1 us  [shards(): coords = coords.reshape(-1)]
    dot_general x4 -> x0, local copies, waits for them, and re-layouts: 13.4 us -> none  [the longest x2 11 us: tile_block(): jnp.einsum('kij,kjf->kif', tile_vals, gathered, precision=lax.Precision.H...]
    gather x3 -> x0, local copies, waits for them, and re-layouts: 8.73 us -> none  [tile_block(): gathered = hblocks[col_index]]
where the time goes in v1:
time: 262 us
  blocking collectives  233 us (89%)
  Pallas kernels  22.6 us (9%)
  local copies, waits for them, and re-layouts  6.33 us (2%)
    all_to_all x4, blocking collectives, exchange(): return lax.all_to_all(x, 'snap', split_axis=0, concat_axis=0, tiled=True)  233 us
    pallas_call x4, Pallas kernels, call(): pl.pallas_call(kernel, out_shape=out_shape, in_specs=in_specs, out_specs=...  22.6 us
    unnamed x14, local copies, waits for them, and re-layouts  6.22 us

profile of v1, /device:TPU:6, one launch (start us, length us, event | category | flops | bytes accessed | tf_op | source)
XLA Modules:
  0.0 262.1 jit_solution(4902626803409301043)
XLA Ops:
  0.0 0.8 copy.8
  0.8 0.1 reshape.15.coords
  0.9 0.0 copy-start
  0.9 1.6 copy-done
  2.5 0.0 copy-start.1
  2.5 1.6 copy-done.1
  4.1 0.0 copy-start.3
  4.1 0.9 copy-done.3
  5.0 4.0 %product.2 = f32[64,32,256]{2,1,0:T(8,128)S(1)} custom-call(s32[64]{0:T(128)S(1)} %reshape.15.coords, f32[2048,256]{1,0:T(8,128)S(1)} %bitcast.5, f32[32,128,128]{2,1,0:T(8,128)S(1)} %bitcast.6, f32[256,256]{1,0:T(8,128)S(1)} %copy-done.3), custom_call_target="tpu_custom_call" | custom-call | flops 3200000000 | bytes 6291456 | tf_op jit(solution)/shard_map/product/pallas_call | solution.py:71
  9.0 0.0 copy-start.5
  9.0 63.3 %all_to_all.20.part = f32[64,32,256]{2,1,0:T(8,128)S(1)} all-to-all(f32[64,32,256]{2,1,0:T(8,128)S(1)} %product.2), channel_id=1, replica_groups=mesh['snap'=64,'rep'=4] {'snap'}, dimensions={0} | all-to-all | bytes 4194304 | tf_op jit(solution)/shard_map/all_to_all | solution.py:103
  72.3 0.0 copy-done.5
  72.3 7.3 %mix.2 = f32[64,32,256]{2,1,0:T(8,128)S(1)} custom-call(f32[64,64]{1,0:T(8,128)S(1)} %copy-done.5, f32[64,32,256]{2,1,0:T(8,128)S(1)} %all_to_all.20.part), custom_call_target="tpu_custom_call" | custom-call | flops 1600000000 | bytes 4194304 | tf_op jit(solution)/shard_map/mix/pallas_call | solution.py:71
  79.6 0.0 copy-start.2
  79.6 0.0 copy-start.4
  79.6 56.6 %all_to_all.21 = f32[64,32,256]{2,1,0:T(8,128)S(1)} all-to-all(f32[64,32,256]{2,1,0:T(8,128)S(1)} %mix.2), channel_id=1, replica_groups=mesh['snap'=64,'rep'=4] {'snap'}, dimensions={0} | all-to-all | bytes 4194304 | tf_op jit(solution)/shard_map/all_to_all | solution.py:103
  136.2 0.0 copy-done.2
  136.2 0.0 copy-done.4
  136.3 4.0 %product.3 = f32[64,32,256]{2,1,0:T(8,128)S(1)} custom-call(s32[64]{0:T(128)S(1)} %reshape.15.coords, f32[2048,256]{1,0:T(8,128)S(1)} %bitcast.4, f32[32,128,128]{2,1,0:T(8,128)S(1)} %bitcast.7, f32[256,256]{1,0:T(8,128)S(1)} %copy-done.4), custom_call_target="tpu_custom_call" | custom-call | flops 3200000000 | bytes 6291456 | tf_op jit(solution)/shard_map/product/pallas_call | solution.py:71
  140.3 56.7 %all_to_all.22.part = f32[64,32,256]{2,1,0:T(8,128)S(1)} all-to-all(f32[64,32,256]{2,1,0:T(8,128)S(1)} %product.3), channel_id=1, replica_groups=mesh['snap'=64,'rep'=4] {'snap'}, dimensions={0} | all-to-all | bytes 4194304 | tf_op jit(solution)/shard_map/all_to_all | solution.py:103
  197.0 7.3 %mix.3 = f32[64,32,256]{2,1,0:T(8,128)S(1)} custom-call(f32[64,64]{1,0:T(8,128)S(1)} %copy-done.5, f32[64,32,256]{2,1,0:T(8,128)S(1)} %all_to_all.22.part), custom_call_target="tpu_custom_call" | custom-call | flops 1600000000 | bytes 4194304 | tf_op jit(solution)/shard_map/mix/pallas_call | solution.py:71
  204.3 56.5 %all_to_all.23 = f32[64,32,256]{2,1,0:T(8,128)S(1)} all-to-all(f32[64,32,256]{2,1,0:T(8,128)S(1)} %mix.3), channel_id=1, replica_groups=mesh['snap'=64,'rep'=4] {'snap'}, dimensions={0} | all-to-all | bytes 4194304 | tf_op jit(solution)/shard_map/all_to_all | solution.py:103
  260.8 1.3 copy.10
Async XLA Ops:
  0.9 1.6 copy-start
  2.5 1.6 copy-start.1
  4.1 0.9 copy-start.3
  9.0 63.3 %copy-start.5 = (f32[64,64]{1,0:T(8,128)S(1)}, f32[64,64]{1,0:T(8,128)}, u32[]{:S(2)}) copy-start(f32[64,64]{1,0:T(8,128)} %mixer.3) | copy-start | bytes 49156
  79.6 56.7 %copy-start.2 = (f32[1,32,128,128]{3,2,1,0:T(8,128)S(1)}, f32[1,32,128,128]{3,2,1,0:T(8,128)}, u32[]{:S(2)}) copy-start(f32[1,32,128,128]{3,2,1,0:T(8,128)} %param.7) | copy-start | bytes 6291460
  79.6 56.6 %copy-start.4 = (f32[256,256]{1,0:T(8,128)S(1)}, f32[256,256]{1,0:T(8,128)}, u32[]{:S(2)}) copy-start(f32[256,256]{1,0:T(8,128)} %weight.3) | copy-start | bytes 786436

commit v2 on v1

v2 whole, which is shorter than its diff:
```python
import jax
import jax.numpy as jnp
from jax import lax
from jax.experimental import pallas as pl
from jax.experimental.pallas import tpu as pltpu
from jax.sharding import PartitionSpec as P

NZ, NYC = 8, 8
SNAPS = NZ * NYC
ORDER = [z * NYC + a for a in range(NYC) for z in range(NZ)]
VERT, FEAT, TILE = 2048, 256, 128
HALF = FEAT // 2
OWN = VERT // SNAPS
NBLK = VERT // TILE
BF, F32 = jnp.bfloat16, jnp.float32
WHOLE = jax.ShapeDtypeStruct((SNAPS, OWN, FEAT), F32)
PARAMS = pltpu.CompilerParams(vmem_limit_bytes=32 << 20)
MOST = pltpu.CompilerParams(vmem_limit_bytes=60 << 20)
VSPEC = pl.BlockSpec(memory_space=pltpu.VMEM)
SSPEC = pl.BlockSpec(memory_space=pltpu.SMEM)
FAR = pl.BlockSpec(memory_space=pl.ANY)


def split(x):
    hi = x.astype(BF)
    return hi, (x - hi.astype(F32)).astype(BF)


def dot(a, b):
    return jnp.dot(a, b, preferred_element_type=F32)


def put_block(pair, h, blk, value):
    hi, lo = split(value)
    both = jnp.concatenate([hi, lo], axis=1)
    pair[h, blk, :TILE] = both
    pair[h, blk, TILE:] = both


def weigh_rows(rows, w_split, pair, r):
    w_hi, w_lo = w_split
    s_hi, s_lo = split(rows)
    u = dot(s_hi, w_hi) + (dot(s_hi, w_lo) + dot(s_lo, w_hi))
    for q in range(0, rows.shape[0], TILE):
        for h in range(2):
            put_block(pair, h, (r + q) // TILE, u[q : q + TILE, h * HALF : (h + 1) * HALF])


def add_tile(coords, k, tile, pair, acc):
    row = coords[0, k]
    used = row >= 0
    row = jnp.where(used, row, NBLK)
    col = jnp.where(used, coords[1, k], 0)
    lhs = jnp.concatenate(split(tile), axis=1)
    for h in range(2):
        wide = dot(lhs, pair[h, col])
        acc[row, :, h * HALF : (h + 1) * HALF] += wide[:, :HALF] + wide[:, HALF:]


def finish(acc, out):
    out[...] = acc[:NBLK].reshape(SNAPS, OWN, FEAT)


def product_kernel(coords, state, tiles, weight, out, pair, acc):
    w_split = split(weight[...])
    acc[...] = jnp.zeros_like(acc)
    for r in range(0, VERT, CHUNK):
        weigh_rows(state[r : r + CHUNK, :], w_split, pair, r)
    for k in range(tiles.shape[0]):
        add_tile(coords, k, tiles[k], pair, acc)
    finish(acc, out)


def loading_kernel(coords, state_far, tiles_far, weight_far, out, pair, acc, state, tiles, weight, sems):
    count = tiles.shape[0]
    step = count // PIECES
    copies = [pltpu.make_async_copy(weight_far, weight, sems.at[0])]
    for i in range(VERT // CHUNK):
        rows = pl.ds(i * CHUNK, CHUNK)
        copies.append(pltpu.make_async_copy(state_far.at[rows], state.at[rows], sems.at[len(copies)]))
    for i in range(PIECES):
        part = pl.ds(i * step, step)
        copies.append(pltpu.make_async_copy(tiles_far.at[part], tiles.at[part], sems.at[len(copies)]))
    for copy in copies:
        copy.start()
    acc[...] = jnp.zeros_like(acc)
    copies[0].wait()
    w_split = split(weight[...])
    for i in range(VERT // CHUNK):
        copies[1 + i].wait()
        weigh_rows(state[i * CHUNK : (i + 1) * CHUNK, :], w_split, pair, i * CHUNK)
    for i in range(PIECES):
        copies[1 + VERT // CHUNK + i].wait()
        for k in range(i * step, (i + 1) * step):
            add_tile(coords, k, tiles[k], pair, acc)
    finish(acc, out)


CHUNK, PIECES = 256, 4
SCRATCH = [pltpu.VMEM((2, NBLK, 2 * TILE, FEAT), BF), pltpu.VMEM((NBLK + 1, TILE, FEAT), F32)]


def cost(flops, moved):
    return pl.CostEstimate(flops=flops, bytes_accessed=moved, transcendentals=0)


def call(kernel, name, out_shape, in_specs, scratch, flops, moved, *args, params=PARAMS):
    return pl.pallas_call(
        kernel,
        out_shape=out_shape,
        in_specs=in_specs,
        out_specs=jax.tree.map(lambda _: VSPEC, out_shape),
        scratch_shapes=scratch,
        compiler_params=params,
        cost_estimate=cost(flops, moved),
        name=name,
    )(*args)


def product(coords, state, tiles, weight):
    return call(
        product_kernel, "product", WHOLE, [SSPEC, VSPEC, VSPEC, VSPEC], SCRATCH,
        3_200_000_000, 6 << 20, coords, state, tiles, weight,
    )


def loading_product(coords, state, tiles, weight):
    near = [pltpu.VMEM(x.shape, F32) for x in (state, tiles, weight)]
    sems = [pltpu.SemaphoreType.DMA((1 + VERT // CHUNK + PIECES,))]
    return call(
        loading_kernel, "loading_product", WHOLE, [SSPEC, FAR, FAR, FAR], SCRATCH + near + sems,
        3_200_000_000, 6 << 20, coords, state, tiles, weight, params=MOST,
    )


def mix_kernel(mixer, part, out):
    place = lax.broadcasted_iota(jnp.int32, (SNAPS, SNAPS), 0)
    snap = lax.broadcasted_iota(jnp.int32, (SNAPS, SNAPS), 1)
    pick = (lax.rem(place, NZ) * NYC + lax.div(place, NZ) == snap).astype(F32).astype(BF)

    def reorder(t):
        rows = dot(pick, t).astype(BF)
        return lax.dot_general(rows, pick, (((1,), (1,)), ((), ())), preferred_element_type=F32).astype(BF)

    t_hi, t_lo = [reorder(t) for t in split(mixer[...])]
    lhs = jnp.concatenate([t_hi, t_lo, t_hi, t_lo], axis=1)
    for h in range(2):
        cols = slice(h * HALF, (h + 1) * HALF)
        for i in range(0, OWN, 2):
            hi, lo = split(jnp.concatenate([part[:, i, cols], part[:, i + 1, cols]], axis=1))
            mixed = jnp.tanh(dot(lhs, jnp.concatenate([hi, hi, lo, lo], axis=0)))
            out[:, i, cols] = mixed[:, :HALF]
            out[:, i + 1, cols] = mixed[:, HALF:]


def mix(mixer, part):
    return call(mix_kernel, "mix", WHOLE, [VSPEC] * 2, [], 1_600_000_000, 4 << 20, mixer, part)


def exchange(x):
    return lax.all_to_all(x, "snap", split_axis=0, concat_axis=0, tiled=True, axis_index_groups=[ORDER])


def shards(features, tiles, coords, temporal, weight_one, weight_two):
    tiles = tiles.reshape(tiles.shape[1:])
    coords = coords[0].T
    mine = loading_product(coords, features.reshape(VERT, FEAT), tiles, weight_one)
    state = exchange(mix(temporal, exchange(mine)))
    mine = product(coords, state.reshape(VERT, FEAT), tiles, weight_two)
    return exchange(mix(temporal, exchange(mine))).reshape(features.shape)


def solution(mesh):
    return jax.shard_map(
        shards,
        mesh=mesh,
        in_specs=(
            P("snap", "rep", None),
            P("snap", "rep", None, None),
            P("snap", "rep", None),
            P(),
            P(),
            P(),
        ),
        out_specs=P("snap", "rep", None),
        check_vma=False,
    )
```

time: 262 us -> 254 us (0.969); the launches traced: 262 us -> 251 us
  Pallas kernels: 22.6 us -> 16 us
  local copies, waits for them, and re-layouts: 6.33 us -> 1.34 us
    pallas_call x4, Pallas kernels: 22.6 us -> 16 us  [call(): pl.pallas_call(kernel, out_shape=out_shape, in_specs=in_specs, out_specs=...]
    unnamed x14 -> x9, local copies, waits for them, and re-layouts: 6.22 us -> 1.34 us
where the time goes in v2:
time: 254 us; the launch traced here: 251 us
  blocking collectives  234 us (92%)
  Pallas kernels  16 us (6%)
    all_to_all x4, blocking collectives, exchange(): lax.all_to_all(x, 'snap', split_axis=0, concat_axis=0, tiled=True, axis_i...  234 us
    pallas_call x4, Pallas kernels, call(): pl.pallas_call(kernel, out_shape=out_shape, in_specs=in_specs, out_specs=...  16 us

profile of v2, /device:TPU:6, one launch (start us, length us, event | category | flops | bytes accessed | tf_op | source)
XLA Modules:
  0.0 251.2 jit_solution(8486564575133282693)
XLA Ops:
  0.0 8.0 %loading_product.1 = f32[64,32,256]{2,1,0:T(8,128)} custom-call(s32[2,32]{1,0:T(2,128)} %bitcast.10, f32[2048,256]{1,0:T(8,128)} %bitcast.13, f32[32,128,128]{2,1,0:T(8,128)} %bitcast.8, f32[256,256]{1,0:T(8,128)} %weight_far.1), custom_call_target="tpu_custom_call" | custom-call | flops 3200000000 | bytes 6291456 | tf_op jit(solution)/shard_map/loading_product/pallas_call | solution.py:108
  8.0 0.0 copy-start.2
  8.0 62.1 %all_to_all.20.part = f32[64,32,256]{2,1,0:T(8,128)S(1)} all-to-all(f32[64,32,256]{2,1,0:T(8,128)} %loading_product.1), channel_id=1, replica_groups={{0,32,64,96,128,160,192,224,4,36,68,100,132,164,196,228,8,40,72,104,136..., dimensions={0} | all-to-all | bytes 4194304 | tf_op jit(solution)/shard_map/all_to_all | solution.py:161
  70.1 0.0 copy-done.2
  70.1 2.5 mix.2
  72.6 0.0 copy-start
  72.6 0.0 copy-start.1
  72.6 0.0 copy-start.3
  72.6 57.3 %all_to_all.21 = f32[64,32,256]{2,1,0:T(8,128)S(1)} all-to-all(f32[64,32,256]{2,1,0:T(8,128)S(1)} %mix.2), channel_id=1, replica_groups={{0,32,64,96,128,160,192,224,4,36,68,100,132,164,196,228,8,40,72,104,136..., dimensions={0} | all-to-all | bytes 4194304 | tf_op jit(solution)/shard_map/all_to_all | solution.py:161
  129.9 0.0 copy-done
  129.9 0.0 copy-done.1
  129.9 0.0 copy-done.3
  129.9 3.1 %product.1 = f32[64,32,256]{2,1,0:T(8,128)S(1)} custom-call(s32[2,32]{1,0:T(2,128)S(1)} %bitcast.11, f32[2048,256]{1,0:T(8,128)S(1)} %bitcast.7, f32[32,128,128]{2,1,0:T(8,128)S(1)} %bitcast.9, f32[256,256]{1,0:T(8,128)S(1)} %copy-done.1), custom_call_target="tpu_custom_call" | custom-call | flops 3200000000 | bytes 6291456 | tf_op jit(solution)/shard_map/product/pallas_call | solution.py:108
  133.0 57.2 %all_to_all.22.part = f32[64,32,256]{2,1,0:T(8,128)S(1)} all-to-all(f32[64,32,256]{2,1,0:T(8,128)S(1)} %product.1), channel_id=1, replica_groups={{0,32,64,96,128,160,192,224,4,36,68,100,132,164,196,228,8,40,72,104,136..., dimensions={0} | all-to-all | bytes 4194304 | tf_op jit(solution)/shard_map/all_to_all | solution.py:161
  190.2 2.5 mix.3
  192.7 57.2 %all_to_all.23 = f32[64,32,256]{2,1,0:T(8,128)S(1)} all-to-all(f32[64,32,256]{2,1,0:T(8,128)S(1)} %mix.3), channel_id=1, replica_groups={{0,32,64,96,128,160,192,224,4,36,68,100,132,164,196,228,8,40,72,104,136..., dimensions={0} | all-to-all | bytes 4194304 | tf_op jit(solution)/shard_map/all_to_all | solution.py:161
  249.9 1.3 copy.8
Async XLA Ops:
  8.0 62.1 %copy-start.2 = (f32[64,64]{1,0:T(8,128)S(1)}, f32[64,64]{1,0:T(8,128)}, u32[]{:S(2)}) copy-start(f32[64,64]{1,0:T(8,128)} %mixer.3) | copy-start | bytes 49156
  72.6 57.4 %copy-start = (f32[1,32,128,128]{3,2,1,0:T(8,128)S(1)}, f32[1,32,128,128]{3,2,1,0:T(8,128)}, u32[]{:S(2)}) copy-start(f32[1,32,128,128]{3,2,1,0:T(8,128)} %param.7) | copy-start | bytes 6291460
  72.6 57.3 %copy-start.1 = (f32[256,256]{1,0:T(8,128)S(1)}, f32[256,256]{1,0:T(8,128)}, u32[]{:S(2)}) copy-start(f32[256,256]{1,0:T(8,128)} %weight.1) | copy-start | bytes 786436
  72.6 57.3 %copy-start.3 = (s32[1,32,2]{1,2,0:T(2,128)S(1)}, s32[1,32,2]{1,2,0:T(2,128)}, u32[]{:S(2)}) copy-start(s32[1,32,2]{1,2,0:T(2,128)} %param.8) | copy-start | bytes 772

commit v3 on v2

--- a/solution.py
+++ b/solution.py
@@ -5,9 +5,7 @@
 from jax.experimental.pallas import tpu as pltpu
 from jax.sharding import PartitionSpec as P
 
-NZ, NYC = 8, 8
-SNAPS = NZ * NYC
-ORDER = [z * NYC + a for a in range(NYC) for z in range(NZ)]
+SNAPS = 64
 VERT, FEAT, TILE = 2048, 256, 128
 HALF = FEAT // 2
 OWN = VERT // SNAPS
@@ -71,26 +69,39 @@
     finish(acc, out)
 
 
-def loading_kernel(coords, state_far, tiles_far, weight_far, out, pair, acc, state, tiles, weight, sems):
+def loading_kernel(
+    coords_far, state_far, tiles_far, weight_far, out, pair, acc, state, tiles, weight, coords, sems
+):
     count = tiles.shape[0]
-    step = count // PIECES
-    copies = [pltpu.make_async_copy(weight_far, weight, sems.at[0])]
-    for i in range(VERT // CHUNK):
-        rows = pl.ds(i * CHUNK, CHUNK)
-        copies.append(pltpu.make_async_copy(state_far.at[rows], state.at[rows], sems.at[len(copies)]))
-    for i in range(PIECES):
-        part = pl.ds(i * step, step)
-        copies.append(pltpu.make_async_copy(tiles_far.at[part], tiles.at[part], sems.at[len(copies)]))
-    for copy in copies:
+    chunks, step = VERT // CHUNK, count // PIECES
+    first = [
+        pltpu.make_async_copy(weight_far, weight, sems.at[0]),
+        pltpu.make_async_copy(coords_far, coords, sems.at[1]),
+    ]
+    states = [
+        pltpu.make_async_copy(state_far.at[pl.ds(i * CHUNK, CHUNK)], state.at[pl.ds(i * CHUNK, CHUNK)], sems.at[2 + i])
+        for i in range(chunks)
+    ]
+    lists = [
+        pltpu.make_async_copy(
+            tiles_far.at[pl.ds(i * step, step)], tiles.at[pl.ds(i * step, step)], sems.at[2 + chunks + i]
+        )
+        for i in range(PIECES)
+    ]
+    for copy in first + states:
         copy.start()
     acc[...] = jnp.zeros_like(acc)
-    copies[0].wait()
+    first[0].wait()
     w_split = split(weight[...])
-    for i in range(VERT // CHUNK):
-        copies[1 + i].wait()
+    for i in range(chunks):
+        states[i].wait()
+        if i % 2 == 0:
+            for copy in lists[i // 2 :: chunks // 2]:
+                copy.start()
         weigh_rows(state[i * CHUNK : (i + 1) * CHUNK, :], w_split, pair, i * CHUNK)
+    first[1].wait()
     for i in range(PIECES):
-        copies[1 + VERT // CHUNK + i].wait()
+        lists[i].wait()
         for k in range(i * step, (i + 1) * step):
             add_tile(coords, k, tiles[k], pair, acc)
     finish(acc, out)
@@ -125,24 +136,16 @@
 
 
 def loading_product(coords, state, tiles, weight):
-    near = [pltpu.VMEM(x.shape, F32) for x in (state, tiles, weight)]
-    sems = [pltpu.SemaphoreType.DMA((1 + VERT // CHUNK + PIECES,))]
+    near = [pltpu.VMEM(x.shape, F32) for x in (state, tiles, weight)] + [pltpu.SMEM(coords.shape, jnp.int32)]
+    sems = [pltpu.SemaphoreType.DMA((2 + VERT // CHUNK + PIECES,))]
     return call(
-        loading_kernel, "loading_product", WHOLE, [SSPEC, FAR, FAR, FAR], SCRATCH + near + sems,
+        loading_kernel, "loading_product", WHOLE, [FAR, FAR, FAR, FAR], SCRATCH + near + sems,
         3_200_000_000, 6 << 20, coords, state, tiles, weight, params=MOST,
     )
 
 
 def mix_kernel(mixer, part, out):
-    place = lax.broadcasted_iota(jnp.int32, (SNAPS, SNAPS), 0)
-    snap = lax.broadcasted_iota(jnp.int32, (SNAPS, SNAPS), 1)
-    pick = (lax.rem(place, NZ) * NYC + lax.div(place, NZ) == snap).astype(F32).astype(BF)
-
-    def reorder(t):
-        rows = dot(pick, t).astype(BF)
-        return lax.dot_general(rows, pick, (((1,), (1,)), ((), ())), preferred_element_type=F32).astype(BF)
-
-    t_hi, t_lo = [reorder(t) for t in split(mixer[...])]
+    t_hi, t_lo = split(mixer[...])
     lhs = jnp.concatenate([t_hi, t_lo, t_hi, t_lo], axis=1)
     for h in range(2):
         cols = slice(h * HALF, (h + 1) * HALF)
@@ -158,7 +161,7 @@
 
 
 def exchange(x):
-    return lax.all_to_all(x, "snap", split_axis=0, concat_axis=0, tiled=True, axis_index_groups=[ORDER])
+    return lax.all_to_all(x, "snap", split_axis=0, concat_axis=0, tiled=True)
 
 
 def shards(features, tiles, coords, temporal, weight_one, weight_two):

time: 254 us -> 250 us (0.984)
  no operation moved by 1% of the time
where the time goes in v3:
time: 250 us; the launch traced here: 249 us
  blocking collectives  233 us (93%)
  Pallas kernels  15 us (6%)
    all_to_all x4, blocking collectives, exchange(): return lax.all_to_all(x, 'snap', split_axis=0, concat_axis=0, tiled=True)  233 us
    pallas_call x4, Pallas kernels, call(): pl.pallas_call(kernel, out_shape=out_shape, in_specs=in_specs, out_specs=...  15 us

profile of v3, /device:TPU:6, one launch (start us, length us, event | category | flops | bytes accessed | tf_op | source)
XLA Modules:
  0.0 249.5 jit_solution(15654286956643068996)
XLA Ops:
  0.0 7.3 %loading_product.1 = f32[64,32,256]{2,1,0:T(8,128)} custom-call(s32[2,32]{1,0:T(2,128)} %bitcast.10, f32[2048,256]{1,0:T(8,128)} %bitcast.13, f32[32,128,128]{2,1,0:T(8,128)} %bitcast.8, f32[256,256]{1,0:T(8,128)} %weight_far.1), custom_call_target="tpu_custom_call" | custom-call | flops 3200000000 | bytes 6291456 | tf_op jit(solution)/shard_map/loading_product/pallas_call | solution.py:119
  7.3 0.0 copy-start.2
  7.3 63.5 %all_to_all.20.part = f32[64,32,256]{2,1,0:T(8,128)S(1)} all-to-all(f32[64,32,256]{2,1,0:T(8,128)} %loading_product.1), channel_id=1, replica_groups=mesh['snap'=64,'rep'=4] {'snap'}, dimensions={0} | all-to-all | bytes 4194304 | tf_op jit(solution)/shard_map/all_to_all | solution.py:164
  70.8 0.0 copy-done.2
  70.8 2.3 mix.2
  73.1 0.0 copy-start
  73.1 0.0 copy-start.1
  73.1 0.0 copy-start.3
  73.1 56.6 %all_to_all.21 = f32[64,32,256]{2,1,0:T(8,128)S(1)} all-to-all(f32[64,32,256]{2,1,0:T(8,128)S(1)} %mix.2), channel_id=1, replica_groups=mesh['snap'=64,'rep'=4] {'snap'}, dimensions={0} | all-to-all | bytes 4194304 | tf_op jit(solution)/shard_map/all_to_all | solution.py:164
  129.7 0.0 copy-done
  129.7 0.0 copy-done.1
  129.8 0.0 copy-done.3
  129.8 3.1 %product.1 = f32[64,32,256]{2,1,0:T(8,128)S(1)} custom-call(s32[2,32]{1,0:T(2,128)S(1)} %bitcast.11, f32[2048,256]{1,0:T(8,128)S(1)} %bitcast.7, f32[32,128,128]{2,1,0:T(8,128)S(1)} %bitcast.9, f32[256,256]{1,0:T(8,128)S(1)} %copy-done.1), custom_call_target="tpu_custom_call" | custom-call | flops 3200000000 | bytes 6291456 | tf_op jit(solution)/shard_map/product/pallas_call | solution.py:119
  132.9 56.5 %all_to_all.22.part = f32[64,32,256]{2,1,0:T(8,128)S(1)} all-to-all(f32[64,32,256]{2,1,0:T(8,128)S(1)} %product.1), channel_id=1, replica_groups=mesh['snap'=64,'rep'=4] {'snap'}, dimensions={0} | all-to-all | bytes 4194304 | tf_op jit(solution)/shard_map/all_to_all | solution.py:164
  189.3 2.3 mix.3
  191.7 56.5 %all_to_all.23 = f32[64,32,256]{2,1,0:T(8,128)S(1)} all-to-all(f32[64,32,256]{2,1,0:T(8,128)S(1)} %mix.3), channel_id=1, replica_groups=mesh['snap'=64,'rep'=4] {'snap'}, dimensions={0} | all-to-all | bytes 4194304 | tf_op jit(solution)/shard_map/all_to_all | solution.py:164
  248.1 1.3 copy.8
Async XLA Ops:
  7.3 63.5 %copy-start.2 = (f32[64,64]{1,0:T(8,128)S(1)}, f32[64,64]{1,0:T(8,128)}, u32[]{:S(2)}) copy-start(f32[64,64]{1,0:T(8,128)} %mixer.3) | copy-start | bytes 49156
  73.1 56.7 %copy-start = (f32[1,32,128,128]{3,2,1,0:T(8,128)S(1)}, f32[1,32,128,128]{3,2,1,0:T(8,128)}, u32[]{:S(2)}) copy-start(f32[1,32,128,128]{3,2,1,0:T(8,128)} %param.7) | copy-start | bytes 6291460
  73.1 56.7 %copy-start.1 = (f32[256,256]{1,0:T(8,128)S(1)}, f32[256,256]{1,0:T(8,128)}, u32[]{:S(2)}) copy-start(f32[256,256]{1,0:T(8,128)} %weight.1) | copy-start | bytes 786436
  73.1 56.6 %copy-start.3 = (s32[1,32,2]{1,2,0:T(2,128)S(1)}, s32[1,32,2]{1,2,0:T(2,128)}, u32[]{:S(2)}) copy-start(s32[1,32,2]{1,2,0:T(2,128)} %param.8) | copy-start | bytes 772

commit v4 on v3

--- a/solution.py
+++ b/solution.py
@@ -70,7 +70,7 @@
 
 
 def loading_kernel(
-    coords_far, state_far, tiles_far, weight_far, out, pair, acc, state, tiles, weight, coords, sems
+    coords_far, state_far, tiles_far, weight_far, out_far, pair, acc, state, tiles, weight, coords, sems
 ):
     count = tiles.shape[0]
     chunks, step = VERT // CHUNK, count // PIECES
@@ -88,23 +88,34 @@
         )
         for i in range(PIECES)
     ]
-    for copy in first + states:
+    sends = [
+        pltpu.make_async_copy(
+            state.at[pl.ds(i * CHUNK, CHUNK)], out_far.at[pl.ds(i * CHUNK, CHUNK)], sems.at[2 + chunks + PIECES + i]
+        )
+        for i in range(chunks)
+    ]
+    for copy in first + states + lists:
         copy.start()
     acc[...] = jnp.zeros_like(acc)
-    first[0].wait()
-    w_split = split(weight[...])
     for i in range(chunks):
         states[i].wait()
-        if i % 2 == 0:
-            for copy in lists[i // 2 :: chunks // 2]:
-                copy.start()
-        weigh_rows(state[i * CHUNK : (i + 1) * CHUNK, :], w_split, pair, i * CHUNK)
+        for blk in range(i * CHUNK // TILE, (i + 1) * CHUNK // TILE):
+            for h in range(2):
+                put_block(pair, h, blk, state[blk * TILE : (blk + 1) * TILE, h * HALF : (h + 1) * HALF])
     first[1].wait()
     for i in range(PIECES):
         lists[i].wait()
         for k in range(i * step, (i + 1) * step):
             add_tile(coords, k, tiles[k], pair, acc)
-    finish(acc, out)
+    first[0].wait()
+    w_hi, w_lo = split(weight[...])
+    for i in range(chunks):
+        blks = slice(i * CHUNK // TILE, (i + 1) * CHUNK // TILE)
+        s_hi, s_lo = split(acc[blks].reshape(CHUNK, FEAT))
+        state[i * CHUNK : (i + 1) * CHUNK, :] = dot(s_hi, w_hi) + (dot(s_hi, w_lo) + dot(s_lo, w_hi))
+        sends[i].start()
+    for copy in sends:
+        copy.wait()
 
 
 CHUNK, PIECES = 256, 4
@@ -115,12 +126,12 @@
     return pl.CostEstimate(flops=flops, bytes_accessed=moved, transcendentals=0)
 
 
-def call(kernel, name, out_shape, in_specs, scratch, flops, moved, *args, params=PARAMS):
+def call(kernel, name, out_shape, in_specs, scratch, flops, moved, *args, params=PARAMS, out_spec=VSPEC):
     return pl.pallas_call(
         kernel,
         out_shape=out_shape,
         in_specs=in_specs,
-        out_specs=jax.tree.map(lambda _: VSPEC, out_shape),
+        out_specs=out_spec,
         scratch_shapes=scratch,
         compiler_params=params,
         cost_estimate=cost(flops, moved),
@@ -137,11 +148,13 @@
 
 def loading_product(coords, state, tiles, weight):
     near = [pltpu.VMEM(x.shape, F32) for x in (state, tiles, weight)] + [pltpu.SMEM(coords.shape, jnp.int32)]
-    sems = [pltpu.SemaphoreType.DMA((2 + VERT // CHUNK + PIECES,))]
-    return call(
-        loading_kernel, "loading_product", WHOLE, [FAR, FAR, FAR, FAR], SCRATCH + near + sems,
-        3_200_000_000, 6 << 20, coords, state, tiles, weight, params=MOST,
+    sems = [pltpu.SemaphoreType.DMA((2 + 2 * VERT // CHUNK + PIECES,))]
+    out = jax.ShapeDtypeStruct((VERT, FEAT), F32)
+    mine = call(
+        loading_kernel, "loading_product", out, [FAR] * 4, SCRATCH + near + sems,
+        3_200_000_000, 6 << 20, coords, state, tiles, weight, params=MOST, out_spec=FAR,
     )
+    return mine.reshape(WHOLE.shape)
 
 
 def mix_kernel(mixer, part, out):

time: 250 us -> 248 us (level)
  no operation moved by 1% of the time
where the time goes in v4:
time: 248 us
  blocking collectives  233 us (94%)
  Pallas kernels  13.4 us (5%)
    all_to_all x4, blocking collectives, exchange(): return lax.all_to_all(x, 'snap', split_axis=0, concat_axis=0, tiled=True)  233 us
    pallas_call x4, Pallas kernels, call(): pl.pallas_call(kernel, out_shape=out_shape, in_specs=in_specs, out_specs=...  13.4 us

profile of v4, /device:TPU:6, one launch (start us, length us, event | category | flops | bytes accessed | tf_op | source)
XLA Modules:
  0.0 247.9 jit_solution(10783787794641149716)
XLA Ops:
  0.0 5.6 %loading_product.1 = f32[2048,256]{1,0:T(8,128)} custom-call(s32[2,32]{1,0:T(2,128)} %bitcast.11, f32[2048,256]{1,0:T(8,128)} %bitcast.15, f32[32,128,128]{2,1,0:T(8,128)} %bitcast.9, f32[256,256]{1,0:T(8,128)} %weight_far.1), custom_call_target="tpu_custom_call" | custom-call | flops 3200000000 | bytes 6291456 | tf_op jit(solution)/shard_map/loading_product/pallas_call | solution.py:130
  5.6 0.0 copy-start.2
  5.6 63.5 %all_to_all.20.part = f32[64,32,256]{2,1,0:T(8,128)S(1)} all-to-all(f32[64,32,256]{2,1,0:T(8,128)} %bitcast.14), channel_id=1, replica_groups=mesh['snap'=64,'rep'=4] {'snap'}, dimensions={0} | all-to-all | bytes 4194304 | tf_op jit(solution)/shard_map/all_to_all | solution.py:177
  69.1 0.0 copy-done.2
  69.1 2.3 mix.2
  71.4 0.0 copy-start
  71.4 0.0 copy-start.1
  71.4 0.0 copy-start.3
  71.4 56.6 %all_to_all.21 = f32[64,32,256]{2,1,0:T(8,128)S(1)} all-to-all(f32[64,32,256]{2,1,0:T(8,128)S(1)} %mix.2), channel_id=1, replica_groups=mesh['snap'=64,'rep'=4] {'snap'}, dimensions={0} | all-to-all | bytes 4194304 | tf_op jit(solution)/shard_map/all_to_all | solution.py:177
  128.1 0.0 copy-done
  128.1 0.0 copy-done.1
  128.1 0.0 copy-done.3
  128.1 3.2 %product.1 = f32[64,32,256]{2,1,0:T(8,128)S(1)} custom-call(s32[2,32]{1,0:T(2,128)S(1)} %bitcast.12, f32[2048,256]{1,0:T(8,128)S(1)} %bitcast.8, f32[32,128,128]{2,1,0:T(8,128)S(1)} %bitcast.10, f32[256,256]{1,0:T(8,128)S(1)} %copy-done.1), custom_call_target="tpu_custom_call" | custom-call | flops 3200000000 | bytes 6291456 | tf_op jit(solution)/shard_map/product/pallas_call | solution.py:130
  131.2 56.5 %all_to_all.22.part = f32[64,32,256]{2,1,0:T(8,128)S(1)} all-to-all(f32[64,32,256]{2,1,0:T(8,128)S(1)} %product.1), channel_id=1, replica_groups=mesh['snap'=64,'rep'=4] {'snap'}, dimensions={0} | all-to-all | bytes 4194304 | tf_op jit(solution)/shard_map/all_to_all | solution.py:177
  187.7 2.3 mix.3
  190.0 56.5 %all_to_all.23 = f32[64,32,256]{2,1,0:T(8,128)S(1)} all-to-all(f32[64,32,256]{2,1,0:T(8,128)S(1)} %mix.3), channel_id=1, replica_groups=mesh['snap'=64,'rep'=4] {'snap'}, dimensions={0} | all-to-all | bytes 4194304 | tf_op jit(solution)/shard_map/all_to_all | solution.py:177
  246.5 1.3 copy.8
Async XLA Ops:
  5.6 63.5 %copy-start.2 = (f32[64,64]{1,0:T(8,128)S(1)}, f32[64,64]{1,0:T(8,128)}, u32[]{:S(2)}) copy-start(f32[64,64]{1,0:T(8,128)} %mixer.3) | copy-start | bytes 49156
  71.4 56.7 %copy-start = (f32[1,32,128,128]{3,2,1,0:T(8,128)S(1)}, f32[1,32,128,128]{3,2,1,0:T(8,128)}, u32[]{:S(2)}) copy-start(f32[1,32,128,128]{3,2,1,0:T(8,128)} %param.7) | copy-start | bytes 6291460
  71.4 56.7 %copy-start.1 = (f32[256,256]{1,0:T(8,128)S(1)}, f32[256,256]{1,0:T(8,128)}, u32[]{:S(2)}) copy-start(f32[256,256]{1,0:T(8,128)} %weight.1) | copy-start | bytes 786436
  71.4 56.7 %copy-start.3 = (s32[1,32,2]{1,2,0:T(2,128)S(1)}, s32[1,32,2]{1,2,0:T(2,128)}, u32[]{:S(2)}) copy-start(s32[1,32,2]{1,2,0:T(2,128)} %param.8) | copy-start | bytes 772

commit v5 on v4

--- a/solution.py
+++ b/solution.py
@@ -160,13 +160,14 @@
 def mix_kernel(mixer, part, out):
     t_hi, t_lo = split(mixer[...])
     lhs = jnp.concatenate([t_hi, t_lo, t_hi, t_lo], axis=1)
-    for h in range(2):
-        cols = slice(h * HALF, (h + 1) * HALF)
-        for i in range(0, OWN, 2):
-            hi, lo = split(jnp.concatenate([part[:, i, cols], part[:, i + 1, cols]], axis=1))
-            mixed = jnp.tanh(dot(lhs, jnp.concatenate([hi, hi, lo, lo], axis=0)))
-            out[:, i, cols] = mixed[:, :HALF]
-            out[:, i + 1, cols] = mixed[:, HALF:]
+    for g in range(0, OWN, 8):
+        rows = slice(g, g + 8)
+        x = jnp.swapaxes(part[:, rows, :], 0, 1)
+        mixed = []
+        for i in range(8):
+            hi, lo = split(x[i])
+            mixed.append(jnp.tanh(dot(lhs, jnp.concatenate([hi, hi, lo, lo], axis=0))))
+        out[:, rows, :] = jnp.swapaxes(jnp.stack(mixed), 0, 1)
 
 
 def mix(mixer, part):

time: 248 us -> 246 us (level)
  no operation moved by 1% of the time
where the time goes in v5:
time: 246 us
  blocking collectives  233 us (95%)
  Pallas kernels  11.6 us (5%)
    all_to_all x4, blocking collectives, exchange(): return lax.all_to_all(x, 'snap', split_axis=0, concat_axis=0, tiled=True)  233 us
    pallas_call x4, Pallas kernels, call(): pl.pallas_call(kernel, out_shape=out_shape, in_specs=in_specs, out_specs=...  11.6 us

profile of v5, /device:TPU:6, one launch (start us, length us, event | category | flops | bytes accessed | tf_op | source)
XLA Modules:
  0.0 246.1 jit_solution(10595287268747452943)
XLA Ops:
  0.0 5.6 %loading_product.1 = f32[2048,256]{1,0:T(8,128)} custom-call(s32[2,32]{1,0:T(2,128)} %bitcast.11, f32[2048,256]{1,0:T(8,128)} %bitcast.15, f32[32,128,128]{2,1,0:T(8,128)} %bitcast.9, f32[256,256]{1,0:T(8,128)} %weight_far.1), custom_call_target="tpu_custom_call" | custom-call | flops 3200000000 | bytes 6291456 | tf_op jit(solution)/shard_map/loading_product/pallas_call | solution.py:130
  5.6 0.0 copy-start.2
  5.6 63.5 %all_to_all.20.part = f32[64,32,256]{2,1,0:T(8,128)S(1)} all-to-all(f32[64,32,256]{2,1,0:T(8,128)} %bitcast.14), channel_id=1, replica_groups=mesh['snap'=64,'rep'=4] {'snap'}, dimensions={0} | all-to-all | bytes 4194304 | tf_op jit(solution)/shard_map/all_to_all | solution.py:178
  69.1 0.0 copy-done.2
  69.1 1.4 mix.2
  70.5 0.0 copy-start
  70.5 0.0 copy-start.1
  70.5 0.0 copy-start.3
  70.5 56.6 %all_to_all.21 = f32[64,32,256]{2,1,0:T(8,128)S(1)} all-to-all(f32[64,32,256]{2,1,0:T(8,128)S(1)} %mix.2), channel_id=1, replica_groups=mesh['snap'=64,'rep'=4] {'snap'}, dimensions={0} | all-to-all | bytes 4194304 | tf_op jit(solution)/shard_map/all_to_all | solution.py:178
  127.2 0.0 copy-done
  127.2 0.0 copy-done.1
  127.2 0.0 copy-done.3
  127.2 3.2 %product.1 = f32[64,32,256]{2,1,0:T(8,128)S(1)} custom-call(s32[2,32]{1,0:T(2,128)S(1)} %bitcast.12, f32[2048,256]{1,0:T(8,128)S(1)} %bitcast.8, f32[32,128,128]{2,1,0:T(8,128)S(1)} %bitcast.10, f32[256,256]{1,0:T(8,128)S(1)} %copy-done.1), custom_call_target="tpu_custom_call" | custom-call | flops 3200000000 | bytes 6291456 | tf_op jit(solution)/shard_map/product/pallas_call | solution.py:130
  130.3 56.5 %all_to_all.22.part = f32[64,32,256]{2,1,0:T(8,128)S(1)} all-to-all(f32[64,32,256]{2,1,0:T(8,128)S(1)} %product.1), channel_id=1, replica_groups=mesh['snap'=64,'rep'=4] {'snap'}, dimensions={0} | all-to-all | bytes 4194304 | tf_op jit(solution)/shard_map/all_to_all | solution.py:178
  186.8 1.4 mix.3
  188.2 56.5 %all_to_all.23 = f32[64,32,256]{2,1,0:T(8,128)S(1)} all-to-all(f32[64,32,256]{2,1,0:T(8,128)S(1)} %mix.3), channel_id=1, replica_groups=mesh['snap'=64,'rep'=4] {'snap'}, dimensions={0} | all-to-all | bytes 4194304 | tf_op jit(solution)/shard_map/all_to_all | solution.py:178
  244.7 1.3 copy.8
Async XLA Ops:
  5.6 63.5 %copy-start.2 = (f32[64,64]{1,0:T(8,128)S(1)}, f32[64,64]{1,0:T(8,128)}, u32[]{:S(2)}) copy-start(f32[64,64]{1,0:T(8,128)} %mixer.3) | copy-start | bytes 49156
  70.5 56.7 %copy-start = (f32[1,32,128,128]{3,2,1,0:T(8,128)S(1)}, f32[1,32,128,128]{3,2,1,0:T(8,128)}, u32[]{:S(2)}) copy-start(f32[1,32,128,128]{3,2,1,0:T(8,128)} %param.7) | copy-start | bytes 6291460
  70.5 56.7 %copy-start.1 = (f32[256,256]{1,0:T(8,128)S(1)}, f32[256,256]{1,0:T(8,128)}, u32[]{:S(2)}) copy-start(f32[256,256]{1,0:T(8,128)} %weight.1) | copy-start | bytes 786436
  70.5 56.6 %copy-start.3 = (s32[1,32,2]{1,2,0:T(2,128)S(1)}, s32[1,32,2]{1,2,0:T(2,128)}, u32[]{:S(2)}) copy-start(s32[1,32,2]{1,2,0:T(2,128)} %param.8) | copy-start | bytes 772

commit v6 on v5

--- a/solution.py
+++ b/solution.py
@@ -35,15 +35,6 @@
     pair[h, blk, TILE:] = both
 
 
-def weigh_rows(rows, w_split, pair, r):
-    w_hi, w_lo = w_split
-    s_hi, s_lo = split(rows)
-    u = dot(s_hi, w_hi) + (dot(s_hi, w_lo) + dot(s_lo, w_hi))
-    for q in range(0, rows.shape[0], TILE):
-        for h in range(2):
-            put_block(pair, h, (r + q) // TILE, u[q : q + TILE, h * HALF : (h + 1) * HALF])
-
-
 def add_tile(coords, k, tile, pair, acc):
     row = coords[0, k]
     used = row >= 0
@@ -59,11 +50,21 @@
     out[...] = acc[:NBLK].reshape(SNAPS, OWN, FEAT)
 
 
-def product_kernel(coords, state, tiles, weight, out, pair, acc):
-    w_split = split(weight[...])
+def put_state(state, pair, blk):
+    for h in range(2):
+        put_block(pair, h, blk, state[blk * TILE : (blk + 1) * TILE, h * HALF : (h + 1) * HALF])
+
+
+def weigh(rows, w_split):
+    w_hi, w_lo = w_split
+    s_hi, s_lo = split(rows)
+    return dot(s_hi, w_hi) + (dot(s_hi, w_lo) + dot(s_lo, w_hi))
+
+
+def sum_kernel(coords, state, tiles, out, pair, acc):
     acc[...] = jnp.zeros_like(acc)
-    for r in range(0, VERT, CHUNK):
-        weigh_rows(state[r : r + CHUNK, :], w_split, pair, r)
+    for blk in range(NBLK):
+        put_state(state, pair, blk)
     for k in range(tiles.shape[0]):
         add_tile(coords, k, tiles[k], pair, acc)
     finish(acc, out)
@@ -100,19 +101,17 @@
     for i in range(chunks):
         states[i].wait()
         for blk in range(i * CHUNK // TILE, (i + 1) * CHUNK // TILE):
-            for h in range(2):
-                put_block(pair, h, blk, state[blk * TILE : (blk + 1) * TILE, h * HALF : (h + 1) * HALF])
+            put_state(state, pair, blk)
     first[1].wait()
     for i in range(PIECES):
         lists[i].wait()
         for k in range(i * step, (i + 1) * step):
             add_tile(coords, k, tiles[k], pair, acc)
     first[0].wait()
-    w_hi, w_lo = split(weight[...])
+    w_split = split(weight[...])
     for i in range(chunks):
         blks = slice(i * CHUNK // TILE, (i + 1) * CHUNK // TILE)
-        s_hi, s_lo = split(acc[blks].reshape(CHUNK, FEAT))
-        state[i * CHUNK : (i + 1) * CHUNK, :] = dot(s_hi, w_hi) + (dot(s_hi, w_lo) + dot(s_lo, w_hi))
+        state[i * CHUNK : (i + 1) * CHUNK, :] = weigh(acc[blks].reshape(CHUNK, FEAT), w_split)
         sends[i].start()
     for copy in sends:
         copy.wait()
@@ -139,10 +138,10 @@
     )(*args)
 
 
-def product(coords, state, tiles, weight):
+def tile_sum(coords, state, tiles):
     return call(
-        product_kernel, "product", WHOLE, [SSPEC, VSPEC, VSPEC, VSPEC], SCRATCH,
-        3_200_000_000, 6 << 20, coords, state, tiles, weight,
+        sum_kernel, "tile_sum", WHOLE, [SSPEC, VSPEC, VSPEC], SCRATCH,
+        1_600_000_000, 6 << 20, coords, state, tiles,
     )
 
 
@@ -157,7 +156,7 @@
     return mine.reshape(WHOLE.shape)
 
 
-def mix_kernel(mixer, part, out):
+def mixed_rows(mixer, part):
     t_hi, t_lo = split(mixer[...])
     lhs = jnp.concatenate([t_hi, t_lo, t_hi, t_lo], axis=1)
     for g in range(0, OWN, 8):
@@ -167,11 +166,29 @@
         for i in range(8):
             hi, lo = split(x[i])
             mixed.append(jnp.tanh(dot(lhs, jnp.concatenate([hi, hi, lo, lo], axis=0))))
-        out[:, rows, :] = jnp.swapaxes(jnp.stack(mixed), 0, 1)
+        yield rows, jnp.stack(mixed)
+
+
+def mix_kernel(mixer, part, out):
+    for rows, mixed in mixed_rows(mixer, part):
+        out[:, rows, :] = jnp.swapaxes(mixed, 0, 1)
+
+
+def mix_weigh_kernel(mixer, weight, part, out):
+    w_split = split(weight[...])
+    for rows, mixed in mixed_rows(mixer, part):
+        done = weigh(mixed.reshape(8 * SNAPS, FEAT), w_split)
+        out[:, rows, :] = jnp.swapaxes(done.reshape(8, SNAPS, FEAT), 0, 1)
 
 
 def mix(mixer, part):
     return call(mix_kernel, "mix", WHOLE, [VSPEC] * 2, [], 1_600_000_000, 4 << 20, mixer, part)
+
+
+def mix_weigh(mixer, weight, part):
+    return call(
+        mix_weigh_kernel, "mix_weigh", WHOLE, [VSPEC] * 3, [], 2_400_000_000, 4 << 20, mixer, weight, part
+    )
 
 
 def exchange(x):
@@ -182,8 +199,8 @@
     tiles = tiles.reshape(tiles.shape[1:])
     coords = coords[0].T
     mine = loading_product(coords, features.reshape(VERT, FEAT), tiles, weight_one)
-    state = exchange(mix(temporal, exchange(mine)))
-    mine = product(coords, state.reshape(VERT, FEAT), tiles, weight_two)
+    state = exchange(mix_weigh(temporal, weight_two, exchange(mine)))
+    mine = tile_sum(coords, state.reshape(VERT, FEAT), tiles)
     return exchange(mix(temporal, exchange(mine))).reshape(features.shape)
 
 

time: 246 us -> 247 us (level)
  no operation moved by 1% of the time
where the time goes in v6:
time: 247 us; the launch traced here: 246 us
  blocking collectives  233 us (94%)
  Pallas kernels  11.6 us (5%)
    all_to_all x4, blocking collectives, exchange(): return lax.all_to_all(x, 'snap', split_axis=0, concat_axis=0, tiled=True)  233 us
    pallas_call x4, Pallas kernels, call(): pl.pallas_call(kernel, out_shape=out_shape, in_specs=in_specs, out_specs=...  11.6 us

profile of v6, /device:TPU:6, one launch (start us, length us, event | category | flops | bytes accessed | tf_op | source)
XLA Modules:
  0.0 246.3 jit_solution(7735475943678507004)
XLA Ops:
  0.0 5.6 %loading_product.1 = f32[2048,256]{1,0:T(8,128)} custom-call(s32[2,32]{1,0:T(2,128)} %bitcast.11, f32[2048,256]{1,0:T(8,128)} %bitcast.15, f32[32,128,128]{2,1,0:T(8,128)} %bitcast.9, f32[256,256]{1,0:T(8,128)} %weight_far.1), custom_call_target="tpu_custom_call" | custom-call | flops 3200000000 | bytes 6291456 | tf_op jit(solution)/shard_map/loading_product/pallas_call | solution.py:129
  5.6 0.0 copy-start.2
  5.6 0.0 copy-start.3
  5.6 63.6 %all_to_all.20.part = f32[64,32,256]{2,1,0:T(8,128)S(1)} all-to-all(f32[64,32,256]{2,1,0:T(8,128)} %bitcast.14), channel_id=1, replica_groups=mesh['snap'=64,'rep'=4] {'snap'}, dimensions={0} | all-to-all | bytes 4194304 | tf_op jit(solution)/shard_map/all_to_all | solution.py:195
  69.2 0.0 copy-done.2
  69.2 0.0 copy-done.3
  69.2 2.2 mix_weigh.1
  71.4 0.0 copy-start
  71.5 0.0 copy-start.1
  71.5 56.6 %all_to_all.21 = f32[64,32,256]{2,1,0:T(8,128)S(1)} all-to-all(f32[64,32,256]{2,1,0:T(8,128)S(1)} %mix_weigh.1), channel_id=1, replica_groups=mesh['snap'=64,'rep'=4] {'snap'}, dimensions={0} | all-to-all | bytes 4194304 | tf_op jit(solution)/shard_map/all_to_all | solution.py:195
  128.1 0.0 copy-done
  128.1 0.0 copy-done.1
  128.1 2.4 tile_sum.1
  130.6 56.5 %all_to_all.22.part = f32[64,32,256]{2,1,0:T(8,128)S(1)} all-to-all(f32[64,32,256]{2,1,0:T(8,128)S(1)} %tile_sum.1), channel_id=1, replica_groups=mesh['snap'=64,'rep'=4] {'snap'}, dimensions={0} | all-to-all | bytes 4194304 | tf_op jit(solution)/shard_map/all_to_all | solution.py:195
  187.1 1.4 mix.1
  188.5 56.5 %all_to_all.23 = f32[64,32,256]{2,1,0:T(8,128)S(1)} all-to-all(f32[64,32,256]{2,1,0:T(8,128)S(1)} %mix.1), channel_id=1, replica_groups=mesh['snap'=64,'rep'=4] {'snap'}, dimensions={0} | all-to-all | bytes 4194304 | tf_op jit(solution)/shard_map/all_to_all | solution.py:195
  245.0 1.3 copy.8
Async XLA Ops:
  5.6 63.6 %copy-start.2 = (f32[256,256]{1,0:T(8,128)S(1)}, f32[256,256]{1,0:T(8,128)}, u32[]{:S(2)}) copy-start(f32[256,256]{1,0:T(8,128)} %weight.1) | copy-start | bytes 786436
  5.6 63.6 %copy-start.3 = (f32[64,64]{1,0:T(8,128)S(1)}, f32[64,64]{1,0:T(8,128)}, u32[]{:S(2)}) copy-start(f32[64,64]{1,0:T(8,128)} %mixer.3) | copy-start | bytes 49156
  71.4 56.6 %copy-start = (f32[1,32,128,128]{3,2,1,0:T(8,128)S(1)}, f32[1,32,128,128]{3,2,1,0:T(8,128)}, u32[]{:S(2)}) copy-start(f32[1,32,128,128]{3,2,1,0:T(8,128)} %param.7) | copy-start | bytes 6291460
  71.5 56.6 %copy-start.1 = (s32[1,32,2]{1,2,0:T(2,128)S(1)}, s32[1,32,2]{1,2,0:T(2,128)}, u32[]{:S(2)}) copy-start(s32[1,32,2]{1,2,0:T(2,128)} %param.8) | copy-start | bytes 772

commit v7 on v6

--- a/solution.py
+++ b/solution.py
@@ -28,22 +28,15 @@
     return jnp.dot(a, b, preferred_element_type=F32)
 
 
-def put_block(pair, h, blk, value):
-    hi, lo = split(value)
-    both = jnp.concatenate([hi, lo], axis=1)
-    pair[h, blk, :TILE] = both
-    pair[h, blk, TILE:] = both
-
-
 def add_tile(coords, k, tile, pair, acc):
     row = coords[0, k]
     used = row >= 0
     row = jnp.where(used, row, NBLK)
     col = jnp.where(used, coords[1, k], 0)
-    lhs = jnp.concatenate(split(tile), axis=1)
-    for h in range(2):
-        wide = dot(lhs, pair[h, col])
-        acc[row, :, h * HALF : (h + 1) * HALF] += wide[:, :HALF] + wide[:, HALF:]
+    a_hi, a_lo = split(tile)
+    high = pair[0, col]
+    both = jnp.concatenate([high, pair[1, col]], axis=0)
+    acc[row] += dot(jnp.concatenate([a_hi, a_hi], axis=1), both) + dot(a_lo, high)
 
 
 def finish(acc, out):
@@ -51,8 +44,7 @@
 
 
 def put_state(state, pair, blk):
-    for h in range(2):
-        put_block(pair, h, blk, state[blk * TILE : (blk + 1) * TILE, h * HALF : (h + 1) * HALF])
+    pair[0, blk], pair[1, blk] = split(state[blk * TILE : (blk + 1) * TILE, :])
 
 
 def weigh(rows, w_split):
@@ -117,8 +109,8 @@
         copy.wait()
 
 
-CHUNK, PIECES = 256, 4
-SCRATCH = [pltpu.VMEM((2, NBLK, 2 * TILE, FEAT), BF), pltpu.VMEM((NBLK + 1, TILE, FEAT), F32)]
+CHUNK, PIECES = 256, 8
+SCRATCH = [pltpu.VMEM((2, NBLK, TILE, FEAT), BF), pltpu.VMEM((NBLK + 1, TILE, FEAT), F32)]
 
 
 def cost(flops, moved):

time: 247 us -> 247 us (level)
  no operation moved by 1% of the time
where the time goes in v7:
time: 247 us
  blocking collectives  233 us (94%)
  Pallas kernels  12.2 us (5%)
    all_to_all x4, blocking collectives, exchange(): return lax.all_to_all(x, 'snap', split_axis=0, concat_axis=0, tiled=True)  233 us
    pallas_call x4, Pallas kernels, call(): pl.pallas_call(kernel, out_shape=out_shape, in_specs=in_specs, out_specs=...  12.2 us

profile of v7, /device:TPU:6, one launch (start us, length us, event | category | flops | bytes accessed | tf_op | source)
XLA Modules:
  0.0 246.8 jit_solution(1069530908214756446)
XLA Ops:
  0.0 6.2 %loading_product.1 = f32[2048,256]{1,0:T(8,128)} custom-call(s32[2,32]{1,0:T(2,128)} %bitcast.11, f32[2048,256]{1,0:T(8,128)} %bitcast.15, f32[32,128,128]{2,1,0:T(8,128)} %bitcast.9, f32[256,256]{1,0:T(8,128)} %weight_far.1), custom_call_target="tpu_custom_call" | custom-call | flops 3200000000 | bytes 6291456 | tf_op jit(solution)/shard_map/loading_product/pallas_call | solution.py:121
  6.2 0.0 copy-start.2
  6.2 0.0 copy-start.3
  6.3 63.6 %all_to_all.20.part = f32[64,32,256]{2,1,0:T(8,128)S(1)} all-to-all(f32[64,32,256]{2,1,0:T(8,128)} %bitcast.14), channel_id=1, replica_groups=mesh['snap'=64,'rep'=4] {'snap'}, dimensions={0} | all-to-all | bytes 4194304 | tf_op jit(solution)/shard_map/all_to_all | solution.py:187
  69.8 0.0 copy-done.2
  69.8 0.0 copy-done.3
  69.8 2.2 mix_weigh.1
  72.0 0.0 copy-start
  72.0 0.0 copy-start.1
  72.1 56.6 %all_to_all.21 = f32[64,32,256]{2,1,0:T(8,128)S(1)} all-to-all(f32[64,32,256]{2,1,0:T(8,128)S(1)} %mix_weigh.1), channel_id=1, replica_groups=mesh['snap'=64,'rep'=4] {'snap'}, dimensions={0} | all-to-all | bytes 4194304 | tf_op jit(solution)/shard_map/all_to_all | solution.py:187
  128.7 0.0 copy-done
  128.7 0.0 copy-done.1
  128.7 2.4 tile_sum.1
  131.1 56.5 %all_to_all.22.part = f32[64,32,256]{2,1,0:T(8,128)S(1)} all-to-all(f32[64,32,256]{2,1,0:T(8,128)S(1)} %tile_sum.1), channel_id=1, replica_groups=mesh['snap'=64,'rep'=4] {'snap'}, dimensions={0} | all-to-all | bytes 4194304 | tf_op jit(solution)/shard_map/all_to_all | solution.py:187
  187.6 1.4 mix.1
  189.0 56.5 %all_to_all.23 = f32[64,32,256]{2,1,0:T(8,128)S(1)} all-to-all(f32[64,32,256]{2,1,0:T(8,128)S(1)} %mix.1), channel_id=1, replica_groups=mesh['snap'=64,'rep'=4] {'snap'}, dimensions={0} | all-to-all | bytes 4194304 | tf_op jit(solution)/shard_map/all_to_all | solution.py:187
  245.5 1.3 copy.8
Async XLA Ops:
  6.2 63.6 %copy-start.2 = (f32[256,256]{1,0:T(8,128)S(1)}, f32[256,256]{1,0:T(8,128)}, u32[]{:S(2)}) copy-start(f32[256,256]{1,0:T(8,128)} %weight.1) | copy-start | bytes 786436
  6.2 63.6 %copy-start.3 = (f32[64,64]{1,0:T(8,128)S(1)}, f32[64,64]{1,0:T(8,128)}, u32[]{:S(2)}) copy-start(f32[64,64]{1,0:T(8,128)} %mixer.3) | copy-start | bytes 49156
  72.0 56.7 %copy-start = (f32[1,32,128,128]{3,2,1,0:T(8,128)S(1)}, f32[1,32,128,128]{3,2,1,0:T(8,128)}, u32[]{:S(2)}) copy-start(f32[1,32,128,128]{3,2,1,0:T(8,128)} %param.7) | copy-start | bytes 6291460
  72.0 56.6 %copy-start.1 = (s32[1,32,2]{1,2,0:T(2,128)S(1)}, s32[1,32,2]{1,2,0:T(2,128)}, u32[]{:S(2)}) copy-start(s32[1,32,2]{1,2,0:T(2,128)} %param.8) | copy-start | bytes 772

commit v8 on v6

--- a/solution.py
+++ b/solution.py
@@ -117,7 +117,7 @@
         copy.wait()
 
 
-CHUNK, PIECES = 256, 4
+CHUNK, PIECES = 128, 4
 SCRATCH = [pltpu.VMEM((2, NBLK, 2 * TILE, FEAT), BF), pltpu.VMEM((NBLK + 1, TILE, FEAT), F32)]
 
 

time: 247 us -> 247 us (level)
  no operation moved by 1% of the time
where the time goes in v8:
time: 247 us; the launch traced here: 246 us
  blocking collectives  233 us (94%)
  Pallas kernels  11.7 us (5%)
    all_to_all x4, blocking collectives, exchange(): return lax.all_to_all(x, 'snap', split_axis=0, concat_axis=0, tiled=True)  233 us
    pallas_call x4, Pallas kernels, call(): pl.pallas_call(kernel, out_shape=out_shape, in_specs=in_specs, out_specs=...  11.7 us

profile of v8, /device:TPU:6, one launch (start us, length us, event | category | flops | bytes accessed | tf_op | source)
XLA Modules:
  0.0 246.3 jit_solution(1373386404039060000)
XLA Ops:
  0.0 5.7 %loading_product.1 = f32[2048,256]{1,0:T(8,128)} custom-call(s32[2,32]{1,0:T(2,128)} %bitcast.11, f32[2048,256]{1,0:T(8,128)} %bitcast.15, f32[32,128,128]{2,1,0:T(8,128)} %bitcast.9, f32[256,256]{1,0:T(8,128)} %weight_far.1), custom_call_target="tpu_custom_call" | custom-call | flops 3200000000 | bytes 6291456 | tf_op jit(solution)/shard_map/loading_product/pallas_call | solution.py:129
  5.7 0.0 copy-start.2
  5.7 0.0 copy-start.3
  5.7 63.6 %all_to_all.20.part = f32[64,32,256]{2,1,0:T(8,128)S(1)} all-to-all(f32[64,32,256]{2,1,0:T(8,128)} %bitcast.14), channel_id=1, replica_groups=mesh['snap'=64,'rep'=4] {'snap'}, dimensions={0} | all-to-all | bytes 4194304 | tf_op jit(solution)/shard_map/all_to_all | solution.py:195
  69.3 0.0 copy-done.2
  69.3 0.0 copy-done.3
  69.3 2.2 mix_weigh.1
  71.5 0.0 copy-start
  71.5 0.0 copy-start.1
  71.5 56.6 %all_to_all.21 = f32[64,32,256]{2,1,0:T(8,128)S(1)} all-to-all(f32[64,32,256]{2,1,0:T(8,128)S(1)} %mix_weigh.1), channel_id=1, replica_groups=mesh['snap'=64,'rep'=4] {'snap'}, dimensions={0} | all-to-all | bytes 4194304 | tf_op jit(solution)/shard_map/all_to_all | solution.py:195
  128.2 0.0 copy-done
  128.2 0.0 copy-done.1
  128.2 2.4 tile_sum.1
  130.6 56.5 %all_to_all.22.part = f32[64,32,256]{2,1,0:T(8,128)S(1)} all-to-all(f32[64,32,256]{2,1,0:T(8,128)S(1)} %tile_sum.1), channel_id=1, replica_groups=mesh['snap'=64,'rep'=4] {'snap'}, dimensions={0} | all-to-all | bytes 4194304 | tf_op jit(solution)/shard_map/all_to_all | solution.py:195
  187.1 1.4 mix.1
  188.5 56.5 %all_to_all.23 = f32[64,32,256]{2,1,0:T(8,128)S(1)} all-to-all(f32[64,32,256]{2,1,0:T(8,128)S(1)} %mix.1), channel_id=1, replica_groups=mesh['snap'=64,'rep'=4] {'snap'}, dimensions={0} | all-to-all | bytes 4194304 | tf_op jit(solution)/shard_map/all_to_all | solution.py:195
  245.0 1.3 copy.8
Async XLA Ops:
  5.7 63.6 %copy-start.2 = (f32[256,256]{1,0:T(8,128)S(1)}, f32[256,256]{1,0:T(8,128)}, u32[]{:S(2)}) copy-start(f32[256,256]{1,0:T(8,128)} %weight.1) | copy-start | bytes 786436
  5.7 63.6 %copy-start.3 = (f32[64,64]{1,0:T(8,128)S(1)}, f32[64,64]{1,0:T(8,128)}, u32[]{:S(2)}) copy-start(f32[64,64]{1,0:T(8,128)} %mixer.3) | copy-start | bytes 49156
  71.5 56.7 %copy-start = (f32[1,32,128,128]{3,2,1,0:T(8,128)S(1)}, f32[1,32,128,128]{3,2,1,0:T(8,128)}, u32[]{:S(2)}) copy-start(f32[1,32,128,128]{3,2,1,0:T(8,128)} %param.7) | copy-start | bytes 6291460
  71.5 56.7 %copy-start.1 = (s32[1,32,2]{1,2,0:T(2,128)S(1)}, s32[1,32,2]{1,2,0:T(2,128)}, u32[]{:S(2)}) copy-start(s32[1,32,2]{1,2,0:T(2,128)} %param.8) | copy-start | bytes 772
